TPU v7x, 128 devices: a whole 4x4x4 slice. The times are simulated.
128 devices in a mesh: req: 8 (over x, core), score: 16 (over y, z).
Axes of the slice: x: 4, y: 4, z: 4, core: 2. Of those that a mesh axis runs over, the one named last changes fastest.
Arguments:
- owner_ids: int32 [8, 16, 4, 256, 1], P('req', 'score'), may hold values from 0 to 127; in each aligned block of 256 rows (0 to 255, 256 to 511, ..., all dimensions but the last counted through in order) at most 3 rows name the same one
- local_rows: int32 [4, 32, 1024], P(None, 'req', 'score'), may hold values from 0 to 16383
- item_table: bfloat16 [2097152, 256], P(('req', 'score')), may hold values from -6 to 6
- user_feats: bfloat16 [4, 32, 1024], P(None, 'req'), may hold values from -6 to 6
- tower_in: bfloat16 [1024, 2048], P(None, 'score'), may hold values from -0.1875 to 0.1875
- tower_out: bfloat16 [2048, 256], P('score'), may hold values from -0.1875 to 0.1875
- cross_weights: bfloat16 [3, 512, 512], replicated, may hold values from -0.25 to 0.25
- mlp_in: bfloat16 [512, 2048], replicated, may hold values from -0.25 to 0.25
- mlp_mid: bfloat16 [2048, 2048], replicated, may hold values from -0.1875 to 0.1875
- mlp_out: bfloat16 [2048], replicated, may hold values from -0.1875 to 0.1875
Outputs:
- logits: float32 [4, 32, 1024], P(None, 'req', 'score')
Inputs may be any that keep to these rules, and one draw needn't show every extreme that they name: Within one window of one device, the 256 candidates of owner_ids[i, j, w] (aligned blocks), no owner is named more than 3 times.
All inputs are finite; a program needn't handle non-finite values.
Results may differ from a plain program's by a relative error of at most 0.013.
Values may be sent and summed in bfloat16 or wider, within the bound.
A program may use at most 128 MiB of HBM per device.

v0:
```python
import jax
import jax.numpy as jnp
from jax import lax
from jax.sharding import PartitionSpec as P

CROSS = 3


def on_device(
    owner_ids,
    local_rows,
    item_table,
    user_feats,
    tower_in,
    tower_out,
    cross_weights,
    mlp_in,
    mlp_mid,
    mlp_out,
):
    req_count = lax.axis_size("req")
    score_count = lax.axis_size("score")
    owners = req_count * score_count
    owner = owner_ids[0, 0, :, :, 0]
    windows, block_rows = owner.shape
    req_rows = local_rows.shape[1]
    cand_rows = local_rows.shape[2]
    slot_most = send_most = max(2, (3 * block_rows + 2 * owners - 1) // (2 * owners))
    columns = jnp.arange(owners, dtype=jnp.int32)
    onehot = (owner[..., None] == columns).astype(jnp.int32)
    before = jnp.cumsum(onehot, axis=1) - onehot
    slot_pos = jnp.sum(before * onehot, axis=-1)
    win_index = jnp.arange(windows, dtype=jnp.int32)[:, None]
    flat_index = ((owner * windows + win_index) * slot_most + slot_pos).reshape(-1)
    send_rows = jnp.full((owners * windows * send_most,), -1, jnp.int32)
    send_rows = (
        send_rows.at[flat_index].set(local_rows.reshape(-1)).reshape(owners, windows, send_most)
    )
    width = item_table.shape[1]
    rows = jnp.take(
        item_table,
        jnp.maximum(
            lax.all_to_all(send_rows, ("req", "score"), split_axis=0, concat_axis=0, tiled=True), 0
        ),
        axis=0,
    )
    returned = lax.all_to_all(rows, ("req", "score"), split_axis=0, concat_axis=0, tiled=True)
    embedded = jnp.take(returned.reshape(-1, width), flat_index, axis=0)
    embedded = embedded.reshape(windows * req_rows, cand_rows, width)
    features = user_feats.shape[-1]
    tower_hidden = jax.nn.relu(
        jnp.dot(
            user_feats.reshape(windows * req_rows, features),
            tower_in,
            preferred_element_type=jnp.float32,
        )
    ).astype(jnp.bfloat16)
    partial_user = jnp.dot(tower_hidden, tower_out, preferred_element_type=jnp.float32)
    user = lax.psum(partial_user, "score").astype(jnp.bfloat16)
    user_rows = jnp.broadcast_to(user[:, None, :], (windows * req_rows, cand_rows, user.shape[-1]))
    base = jnp.concatenate([embedded, user_rows], axis=-1).reshape(
        windows * req_rows * cand_rows, -1
    )
    base_float = base.astype(jnp.float32)
    state = base_float
    for layer in range(CROSS):
        mixed = jnp.dot(
            state.astype(jnp.bfloat16), cross_weights[layer], preferred_element_type=jnp.float32
        )
        state = base_float * mixed + state
    first = jax.nn.relu(
        jnp.dot(state.astype(jnp.bfloat16), mlp_in, preferred_element_type=jnp.float32)
    ).astype(jnp.bfloat16)
    second = jax.nn.relu(jnp.dot(first, mlp_mid, preferred_element_type=jnp.float32)).astype(
        jnp.bfloat16
    )
    logits = jnp.dot(second, mlp_out, preferred_element_type=jnp.float32)
    return logits.reshape(windows, req_rows, cand_rows)


def solution(mesh):
    in_specs = (
        P("req", "score", None, None, None),
        P(None, "req", "score"),
        P(("req", "score"), None),
        P(None, "req", None),
        P(None, "score"),
        P("score", None),
        P(),
        P(),
        P(),
        P(),
    )
    out_specs = P(None, "req", "score")
    return jax.shard_map(
        on_device, mesh=mesh, in_specs=in_specs, out_specs=out_specs, check_vma=False
    )
```

profile of v0, /device:TPU:0, one launch (start us, length us, event | category | flops | bytes accessed | tf_op | source)
XLA Modules:
  0.0 159.3 jit_solution(746819732440913146)
XLA Ops:
  0.0 0.9 copy.24
  0.9 0.7 broadcast_multiply_fusion
  1.6 0.8 copy.14
  2.4 0.9 fusion.10
  3.3 0.2 broadcast_add_fusion
  3.5 0.4 fusion.12
  4.0 0.1 reshape.129
  4.1 4.3 %scatter_custom_fusion = s32[1536]{0:T(1024)S(1)} fusion(s32[1024]{0:T(1024)S(1)} %bitcast.61, s32[1024]{0:T(1024)S(1)} %reshape.129, s32[]{:T(128)} %constant.47.clone.1), kind=kCustom, calls=%fused_computation.45 | custom fusion | bytes 6148 | tf_op jit(solution)/shard_map/scatter | solution.py:37
  8.4 1.0 reshape.105
  9.4 11.1 %all-to-all-start = ((s32[128,4,3]{2,1,0:T(4,128)}), s32[128,4,3]{2,1,0:T(4,128)S(1)}, u32[]{:S(2)}, u32[]{:S(2)}) async-start(s32[128,4,3]{2,1,0:T(4,128)} %reshape.105), calls=%async_computation | async-start | bytes 524288 | tf_op jit(solution)/shard_map/all_to_all | solution.py:43
  20.6 10.9 %all-to-all-done = s32[128,4,3]{2,1,0:T(4,128)S(1)} async-done(((s32[128,4,3]{2,1,0:T(4,128)}), s32[128,4,3]{2,1,0:T(4,128)S(1)}, u32[]{:S(2)}, u32[]{:S(2)}) %all-to-all-start) | async-done | bytes 6176 | tf_op jit(solution)/shard_map/all_to_all | solution.py:43
  31.4 0.1 broadcast_maximum_fusion
  31.5 0.3 reshape.111
  31.8 8.1 %gather_fusion = bf16[1536,256]{1,0:T(8,128)(2,1)S(1)} fusion(bf16[16384,256]{1,0:T(8,128)(2,1)} %param.12, s32[2048]{0:T(1024)S(1)} %pad_clamp_fusion), kind=kCustom, calls=%fused_computation | custom fusion | bytes 1579008 | tf_op jit(solution)/shard_map/jit(_take)/gather | solution.py:40
  39.9 1.2 reshape.110
  41.1 0.1 broadcast_compare_fusion
  41.2 2.6 %broadcast_select_fusion = bf16[128,4,3,256]{3,2,1,0:T(4,128)(2,1)S(1)} fusion(bf16[128,4,3,256]{3,2,1,0:T(4,128)(2,1)} %reshape.110, pred[128,4,3]{2,1,0:T(4,128)(4,1)S(1)} %broadcast_compare_fusion), kind=kLoop, calls=%fused_computation.19 | loop fusion | flops 393216 | bytes 1574400 | tf_op jit(solution)/shard_map/jit(_take)/select_n | solution.py:40
  43.8 0.0 copy-start.3
  43.8 0.0 copy-start.5
  43.9 1.2 copy.16
  45.1 4.6 %all-to-all-start.1 = ((bf16[128,4,3,256]{3,1,2,0:T(4,128)(2,1)}), bf16[128,4,3,256]{3,1,2,0:T(4,128)(2,1)S(1)}, u32[]{:S(2)}, u32[]{:S(2)}) async-start(bf16[128,4,3,256]{3,1,2,0:T(4,128)(2,1)} %copy.16), calls=%async_computation.1 | async-start | bytes 1572864 | tf_op jit(solution)/shard_map/all_to_all | solution.py:47
  49.8 0.3 fusion.5
  50.1 74.8 %psum.7 = bf16[16,256]{1,0:T(8,128)(2,1)S(1)} all-reduce(f32[16,256]{1,0:T(8,128)S(1)} %fusion.5), channel_id=1, replica_groups=mesh['req'=8,'score'=16] {'score'}, use_global_device_ids=true, to_apply=%region_4.5 | all-reduce | flops 4096 | bytes 24576 | tf_op jit(solution)/shard_map/psum | solution.py:59
  124.9 1.4 copy.17
  126.3 2.4 %reshape.106 = bf16[1536,256]{1,0:T(8,128)(2,1)S(1)} reshape(bf16[128,4,3,256]{3,2,1,0:T(4,128)(2,1)} %copy.17) | data formatting | bytes 1572864 | tf_op jit(solution)/shard_map/reshape | solution.py:48
  128.8 3.9 %gather_fusion.1 = bf16[1024,256]{1,0:T(8,128)(2,1)S(1)} fusion(bf16[1536,256]{1,0:T(8,128)(2,1)S(1)} %reshape.106, s32[1024]{0:T(1024)S(1)} %broadcast_clamp_fusion), kind=kCustom, calls=%fused_computation.1 | custom fusion | bytes 1052672 | tf_op jit(solution)/shard_map/jit(_take)/gather | solution.py:48
  132.7 0.2 broadcast_select_fusion.1
  133.0 1.7 %convert_add_fusion = f32[1024,512]{1,0:T(8,128)S(1)} fusion(bf16[3,512,512]{2,1,0:T(8,128)(2,1)} %param.16, bf16[1024,256]{1,0:T(8,128)(2,1)S(1)} %bitcast.50, bf16[1024,256]{1,0:T(8,128)(2,1)S(1)} %broadcast_select_fusion.1), kind=kOutput, calls=%fused_computation.7 | convolution fusion | flops 542113792 | bytes 4718592 | tf_op jit(solution)/shard_map/dot_general | solution.py:67
  134.7 3.1 %fusion = f32[1024,512]{1,0:T(8,128)} fusion(f32[1024,512]{1,0:T(8,128)S(1)} %convert_add_fusion, bf16[3,512,512]{2,1,0:T(8,128)(2,1)} %param.16, bf16[1024,256]{1,0:T(8,128)(2,1)S(1)} %bitcast.51, bf16[1024,256]{1,0:T(8,128)(2,1)S(1)} %broadcast_select_fusion.1), kind=kOutput, calls=%fused_computation.9 | convolution fusion | flops 540540928 | bytes 7864320 | tf_op jit(solution)/shard_map/dot_general | solution.py:67
  137.8 7.4 %maximum_convert_fusion.1 = bf16[1024,2048]{1,0:T(8,128)(2,1)} fusion(bf16[512,2048]{1,0:T(8,128)(2,1)S(1)} %copy-done, f32[1024,512]{1,0:T(8,128)} %fusion, bf16[3,512,512]{2,1,0:T(8,128)(2,1)} %param.16, bf16[1024,256]{1,0:T(8,128)(2,1)S(1)} %bitcast.52, bf16[1024,256]{1,0:T(8,128)(2,1)S(1)} %broadcast_select_fusion.1), kind=kOutput, calls=%fused_computation.4 | convolution fusion | flops 2692743168 | bytes 12058624 | tf_op jit(solution)/shard_map/dot_general | solution.py:72
  145.2 13.4 %fusion.3 = f32[1,1024]{1,0:T(1,128)S(1)} fusion(bf16[2048,1]{0,1:T(2,128)(2,1)S(1)} %reshape.135, bf16[1024,2048]{1,0:T(8,128)(2,1)} %maximum_convert_fusion.1, bf16[2048,2048]{1,0:T(8,128)(2,1)} %param.18), kind=kOutput, calls=%fused_computation.12 | convolution fusion | flops 8598323200 | bytes 12591104 | tf_op jit(solution)/shard_map/dot_general | solution.py:77
  158.6 0.7 reshape.108
  (28 shorter events, 0.2 us)
Async XLA Ops:
  0.0 137.8 %copy-start = (bf16[512,2048]{1,0:T(8,128)(2,1)S(1)}, bf16[512,2048]{1,0:T(8,128)(2,1)}, u32[]{:S(2)}) copy-start(bf16[512,2048]{1,0:T(8,128)(2,1)} %param.17) | copy-start | bytes 6291460
  0.0 4.0 %copy-start.4 = (s32[4,4,64]{2,1,0:T(4,128)S(1)}, s32[4,4,64]{2,1,0:T(4,128)}, u32[]{:S(2)}) copy-start(s32[4,4,64]{2,1,0:T(4,128)} %param.11) | copy-start | bytes 12292
  9.4 22.0 %all-to-all-start = ((s32[128,4,3]{2,1,0:T(4,128)}), s32[128,4,3]{2,1,0:T(4,128)S(1)}, u32[]{:S(2)}, u32[]{:S(2)}) async-start(s32[128,4,3]{2,1,0:T(4,128)} %reshape.105), calls=%async_computation | async-start | bytes 524288 | tf_op jit(solution)/shard_map/all_to_all | solution.py:43
  43.8 5.9 %copy-start.3 = (bf16[4,4,1024]{2,1,0:T(4,128)(2,1)S(1)}, bf16[4,4,1024]{2,1,0:T(4,128)(2,1)}, u32[]{:S(2)}) copy-start(bf16[4,4,1024]{2,1,0:T(4,128)(2,1)} %param.13) | copy-start | bytes 98308
  43.8 5.9 %copy-start.5 = (bf16[2048]{0:T(1024)(128)(2,1)S(1)}, bf16[2048]{0:T(1024)(128)(2,1)}, u32[]{:S(2)}) copy-start(bf16[2048]{0:T(1024)(128)(2,1)} %param.19) | copy-start | bytes 12292
  43.8 6.0 %copy-start.1 = (bf16[1024,128]{1,0:T(8,128)(2,1)S(1)}, bf16[1024,128]{1,0:T(8,128)(2,1)}, u32[]{:S(2)}) copy-start(bf16[1024,128]{1,0:T(8,128)(2,1)} %param.14) | copy-start | bytes 786436
  43.9 6.0 %copy-start.2 = (bf16[128,256]{1,0:T(8,128)(2,1)S(1)}, bf16[128,256]{1,0:T(8,128)(2,1)}, u32[]{:S(2)}) copy-start(bf16[128,256]{1,0:T(8,128)(2,1)} %param.15) | copy-start | bytes 196612
  45.1 79.8 %all-to-all-start.1 = ((bf16[128,4,3,256]{3,1,2,0:T(4,128)(2,1)}), bf16[128,4,3,256]{3,1,2,0:T(4,128)(2,1)S(1)}, u32[]{:S(2)}, u32[]{:S(2)}) async-start(bf16[128,4,3,256]{3,1,2,0:T(4,128)(2,1)} %copy.16), calls=%async_computation.1 | async-start | bytes 1572864 | tf_op jit(solution)/shard_map/all_to_all | solution.py:47
where the time goes:
time: 160 us; the launch traced here: 159 us
  blocking collectives  74.8 us (47%)
  local copies, waits for them, and re-layouts  26.5 us (17%)
  matrix products  25.8 us (16%)
  starting transfers between devices  15.8 us (10%)
  waiting for transfers between devices  10.9 us (7%)
  other arithmetic  5.15 us (3%)
    psum x1, blocking collectives, on_device(): user = lax.psum(partial_user, 'score').astype(jnp.bfloat16)  74.8 us
    dot_general x1, matrix products, on_device(): logits = jnp.dot(second, mlp_out, preferred_element_type=jnp.float32)  13.4 us
    all_to_all x1, starting transfers between devices, on_device(): lax.all_to_all(send_rows, ('req', 'score'), split_axis=0, concat_axis=0,...  11.1 us
    all_to_all x1, waiting for transfers between devices, on_device(): lax.all_to_all(send_rows, ('req', 'score'), split_axis=0, concat_axis=0,...  10.9 us
    gather x2, local copies, waits for them, and re-layouts, on_device(): jnp.take(item_table, jnp.maximum(lax.all_to_all(send_rows, ('req', 'score...  9.31 us
    dot_general x1, matrix products, on_device(): jnp.dot(state.astype(jnp.bfloat16), mlp_in, preferred_element_type=jnp.fl...  7.35 us
    dot_general x2, matrix products, on_device(): jnp.dot(state.astype(jnp.bfloat16), cross_weights[layer], preferred_eleme...  4.85 us
    all_to_all x1, starting transfers between devices, on_device(): lax.all_to_all(rows, ('req', 'score'), split_axis=0, concat_axis=0, tiled...  4.62 us
  transfers between devices with their start and end apart: 2, of which 1 were waited for; matrix products, arithmetic and copies ran while one was open for 0% of the time, Pallas kernels for 0%

commit v1 on v0

v1 whole, which is shorter than its diff:
```python
import functools

import jax
import jax.numpy as jnp
from jax import lax
from jax.experimental import pallas as pl
from jax.experimental.pallas import tpu as pltpu
from jax.sharding import PartitionSpec as P

CROSS = 3
WINDOWS = 4
BLOCK = 256
REQ_ROWS = 4
CAND = 64
MOST = 3
OWNERS = 128
ROWS = 16384
ITEM = 256
USER = 256
HID = 2048
HALF = 2 * BLOCK
SLOTS = 8
USED = 2 * MOST
CHUNKS = 8
MESH = pl.DeviceIdType.MESH
F32 = jnp.float32
BF16 = jnp.bfloat16


def peer(step):
    req, score = lax.axis_index("req"), lax.axis_index("score")
    turn = (step * 37) % 128
    z = (score % 4 + turn % 4) % 4
    y = (score // 4 + (turn // 4) % 4) % 4
    core = (req % 2 + (turn // 16) % 2) % 2
    x = (req // 2 + turn // 32) % 4
    return x * 2 + core, y * 4 + z


def kernel(
    owner_ref, rows_ref, feats_ref, out_w_ref,
    table_hbm, tin_hbm, tout_hbm, cross_hbm, win_hbm, wmid_hbm,
    logits_ref,
    table, table32, tin, tout, cross, win, wmid,
    ask, asked, asked_s, stage, give, got, part, parts, pick, first,
    load_sem, weight_sem, own_sem, ask_send, ask_recv, user_send, user_recv, row_send, row_recv,
):
    req, score = lax.axis_index("req"), lax.axis_index("score")
    me = req * 16 + score
    chunk = ROWS // CHUNKS

    small = [
        pltpu.make_async_copy(tin_hbm, tin, weight_sem.at[0]),
        pltpu.make_async_copy(tout_hbm, tout, weight_sem.at[1]),
    ]
    large = [
        pltpu.make_async_copy(cross_hbm, cross, weight_sem.at[2]),
        pltpu.make_async_copy(win_hbm, win, weight_sem.at[3]),
        pltpu.make_async_copy(wmid_hbm, wmid, weight_sem.at[4]),
    ]
    loads = [
        pltpu.make_async_copy(
            table_hbm.at[pl.ds(k * chunk, chunk)], table.at[pl.ds(k * chunk, chunk)], load_sem.at[k]
        )
        for k in range(CHUNKS)
    ]
    for copy in small + loads + large:
        copy.start()

    barrier = pltpu.get_barrier_semaphore()

    def greet(step, carry):
        to_req, to_score = peer(step)
        pl.semaphore_signal(barrier, inc=1, device_id=(to_req, to_score), device_id_type=MESH)
        return carry

    lax.fori_loop(1, OWNERS, greet, 0)

    tri_row = lax.broadcasted_iota(jnp.int32, (BLOCK, BLOCK), 0)
    tri_col = lax.broadcasted_iota(jnp.int32, (BLOCK, BLOCK), 1)
    earlier = jnp.where(tri_row < tri_col, 1.0, 0.0).astype(BF16)
    owner_iota = lax.broadcasted_iota(jnp.int32, (OWNERS, BLOCK), 0)
    high_sum = jnp.zeros((OWNERS, 128), F32)
    low_sum = jnp.zeros((OWNERS, 128), F32)
    places = []
    for w in range(WINDOWS):
        owner = owner_ref[pl.ds(w, 1), :]
        rows = rows_ref[pl.ds(w, 1), :]
        hot = jnp.where(owner_iota == owner, 1.0, 0.0)
        hot16 = hot.astype(BF16)
        before = jnp.dot(hot16, earlier, preferred_element_type=F32)
        slot = jnp.sum(before * hot, axis=0, keepdims=True).astype(jnp.int32)
        at_slot = owner_iota == slot + w * MOST
        high = jnp.where(at_slot, (rows // 128).astype(F32), 0.0).astype(BF16)
        low = jnp.where(at_slot, (rows % 128).astype(F32), 0.0).astype(BF16)
        contract = (((1,), (1,)), ((), ()))
        high_sum += lax.dot_general(hot16, high, contract, preferred_element_type=F32)
        low_sum += lax.dot_general(hot16, low, contract, preferred_element_type=F32)
        places.append(owner * SLOTS + slot + (w % 2) * MOST)
    asks = (high_sum * 128.0 + low_sum).astype(jnp.int32) * 2
    ask[...] = asks.reshape(OWNERS, 1, 128)

    pl.semaphore_wait(barrier, OWNERS - 1)

    def send_ask(step, carry):
        to_req, to_score = peer(step)
        pltpu.make_async_remote_copy(
            src_ref=ask.at[to_req * 16 + to_score],
            dst_ref=asked.at[me],
            send_sem=ask_send,
            recv_sem=ask_recv,
            device_id=(to_req, to_score),
            device_id_type=MESH,
        ).start()
        return carry

    lax.fori_loop(1, OWNERS, send_ask, 0)
    asked[pl.ds(me, 1)] = ask[pl.ds(me, 1)]

    for copy in small:
        copy.wait()
    feats = jnp.concatenate([feats_ref[w].astype(F32) for w in range(WINDOWS)], axis=0).astype(BF16)
    hidden = jnp.maximum(jnp.dot(feats, tin[...], preferred_element_type=F32), 0.0).astype(BF16)
    part[...] = jnp.dot(hidden, tout[...], preferred_element_type=F32)

    def send_part(step, carry):
        pltpu.make_async_remote_copy(
            src_ref=part,
            dst_ref=parts.at[score],
            send_sem=user_send,
            recv_sem=user_recv,
            device_id=(req, (score + step) % 16),
            device_id_type=MESH,
        ).start()
        return carry

    lax.fori_loop(1, 16, send_part, 0)
    parts[pl.ds(score, 1)] = part[...][None]

    for k in range(CHUNKS):
        loads[k].wait()

        def widen(step, carry):
            base = pl.multiple_of(k * chunk + step * 64, 64)
            block = table[pl.ds(base, 64), :].astype(F32)
            table32[pl.ds(2 * base, 64, stride=2), :] = block[:, :128]
            table32[pl.ds(2 * base + 1, 64, stride=2), :] = block[:, 128:]
            return carry

        lax.fori_loop(0, chunk // 64, widen, 0)

    place = jnp.concatenate(places + [jnp.zeros((4, BLOCK), jnp.int32)], axis=0)
    place_t = place.T
    lane = lax.broadcasted_iota(jnp.int32, (BLOCK, OWNERS * SLOTS), 1)
    for w in range(WINDOWS):
        pick[w * BLOCK:(w + 1) * BLOCK, :] = jnp.where(
            lane == place_t[:, w:w + 1], 1.0, 0.0
        ).astype(BF16)

    everything = asked.at[pl.ds(0, OWNERS - 1)]
    pltpu.make_async_copy(everything, everything, ask_recv).wait()
    to_smem = pltpu.make_async_copy(asked, asked_s, own_sem.at[0])
    to_smem.start()

    def clear(step, carry):
        stage[pl.ds(pl.multiple_of(step * 64, 64), 64), :] = jnp.zeros((64, 128), F32)
        return carry

    lax.fori_loop(0, 2 * OWNERS * 2 * SLOTS // 64, clear, 0)
    to_smem.wait()

    def look_up(half, to):
        base = pl.multiple_of((half * OWNERS + to) * 2 * SLOTS, 2 * SLOTS)
        for s in range(USED):
            at = jnp.clip(asked_s[to, 0, half * USED + s], 0, 2 * ROWS - 2)
            stage[pl.ds(base + 2 * s, 2), :] = table32[pl.ds(at, 2), :]
        give[half, to, 0:SLOTS, :] = stage[pl.ds(base, SLOTS, stride=2), :].astype(BF16)
        give[half, to, SLOTS:2 * SLOTS, :] = stage[pl.ds(base + 1, SLOTS, stride=2), :].astype(BF16)

    for half in range(2):

        def send_rows(step, carry):
            to_req, to_score = peer(step)
            to = to_req * 16 + to_score
            look_up(half, to)
            pltpu.make_async_remote_copy(
                src_ref=give.at[half, to],
                dst_ref=got.at[half, me],
                send_sem=row_send.at[half],
                recv_sem=row_recv.at[half],
                device_id=(to_req, to_score),
                device_id_type=MESH,
            ).start()
            return carry

        lax.fori_loop(1, OWNERS, send_rows, 0)
        look_up(half, me)
        got[half, pl.ds(me, 1)] = give[half, pl.ds(me, 1)]

    fifteen = parts.at[pl.ds(0, 15)]
    pltpu.make_async_copy(fifteen, fifteen, user_recv).wait()
    user = jnp.sum(parts[...], axis=0).astype(BF16)
    for copy in large:
        copy.wait()
    user_mixed = jnp.dot(user, cross[0, ITEM:, :], preferred_element_type=F32)
    user32 = user.astype(F32)

    def spread(rows, half):
        width = rows.shape[1]
        return jnp.concatenate(
            [jnp.broadcast_to(rows[q:q + 1], (CAND, width)) for q in range(8 * half, 8 * half + 8)],
            axis=0,
        )

    for half in range(2):
        arrived = got.at[half, pl.ds(0, OWNERS - 1)]
        pltpu.make_async_copy(arrived, arrived, row_recv.at[half]).wait()
        left = got[half, :, 0:SLOTS, :].reshape(OWNERS * SLOTS, 128)
        right = got[half, :, SLOTS:2 * SLOTS, :].reshape(OWNERS * SLOTS, 128)
        found = jnp.concatenate([left, right], axis=1)
        embedded = jnp.dot(
            pick[half * HALF:(half + 1) * HALF, :], found, preferred_element_type=F32
        )
        base = jnp.concatenate([embedded, spread(user32, half)], axis=1)
        mixed = jnp.dot(
            embedded.astype(BF16), cross[0, :ITEM, :], preferred_element_type=F32
        ) + spread(user_mixed, half)
        state = base * mixed + base
        for layer in range(1, CROSS):
            mixed = jnp.dot(state.astype(BF16), cross[layer], preferred_element_type=F32)
            state = base * mixed + state
        state16 = state.astype(BF16)

        def deep_in(n, carry):
            columns = pl.ds(pl.multiple_of(n * 256, 256), 256)
            value = jnp.dot(state16, win[:, columns], preferred_element_type=F32)
            first[:, columns] = jnp.maximum(value, 0.0).astype(BF16)
            return carry

        lax.fori_loop(0, HID // 256, deep_in, 0)

        def deep_mid(n, total):
            columns = pl.ds(pl.multiple_of(n * 256, 256), 256)
            value = jnp.dot(first[...], wmid[:, columns], preferred_element_type=F32)
            second = jnp.maximum(value, 0.0).astype(BF16).astype(F32) * out_w_ref[:, columns]
            return total + second[:, :128] + second[:, 128:]

        total = lax.fori_loop(0, HID // 256, deep_mid, jnp.zeros((HALF, 128), F32))
        scores = jnp.sum(total.T, axis=0, keepdims=True)
        for q in range(8):
            logits_ref[half * 2 + q // 4, pl.ds(q % 4, 1), :] = scores[:, q * CAND:(q + 1) * CAND]

    pltpu.make_async_copy(everything, everything, ask_send).wait()
    pltpu.make_async_copy(fifteen, fifteen, user_send).wait()
    for half in range(2):
        arrived = got.at[half, pl.ds(0, OWNERS - 1)]
        pltpu.make_async_copy(arrived, arrived, row_send.at[half]).wait()


def on_device(
    owner_ids, local_rows, item_table, user_feats, tower_in, tower_out,
    cross_weights, mlp_in, mlp_mid, mlp_out,
):
    vmem = pl.BlockSpec(memory_space=pltpu.VMEM)
    hbm = pl.BlockSpec(memory_space=pl.ANY)
    dma = pltpu.SemaphoreType.DMA
    return pl.pallas_call(
        kernel,
        out_shape=jax.ShapeDtypeStruct((WINDOWS, REQ_ROWS, CAND), F32),
        in_specs=[vmem] * 4 + [hbm] * 6,
        out_specs=vmem,
        scratch_shapes=[
            pltpu.VMEM((ROWS, ITEM), BF16),
            pltpu.VMEM((2 * ROWS + 8, 128), F32),
            pltpu.VMEM((1024, 128), BF16),
            pltpu.VMEM((128, USER), BF16),
            pltpu.VMEM((CROSS, 512, 512), BF16),
            pltpu.VMEM((512, HID), BF16),
            pltpu.VMEM((HID, HID), BF16),
            pltpu.VMEM((OWNERS, 1, 128), jnp.int32),
            pltpu.VMEM((OWNERS, 1, 128), jnp.int32),
            pltpu.SMEM((OWNERS, 1, 128), jnp.int32),
            pltpu.VMEM((2 * OWNERS * 2 * SLOTS + 8, 128), F32),
            pltpu.VMEM((2, OWNERS, 2 * SLOTS, 128), BF16),
            pltpu.VMEM((2, OWNERS, 2 * SLOTS, 128), BF16),
            pltpu.VMEM((16, USER), F32),
            pltpu.VMEM((16, 16, USER), F32),
            pltpu.VMEM((WINDOWS * BLOCK, OWNERS * SLOTS), BF16),
            pltpu.VMEM((HALF, HID), BF16),
            dma((CHUNKS,)),
            dma((5,)),
            dma((1,)),
            dma,
            dma,
            dma,
            dma,
            dma((2,)),
            dma((2,)),
        ],
        compiler_params=pltpu.CompilerParams(
            collective_id=0, has_side_effects=True, vmem_limit_bytes=60 * 1024 * 1024
        ),
        cost_estimate=pl.CostEstimate(
            flops=13_500_000_000, bytes_accessed=21_000_000, transcendentals=0
        ),
    )(
        owner_ids.reshape(WINDOWS, BLOCK),
        local_rows.reshape(WINDOWS, BLOCK),
        user_feats,
        mlp_out.astype(F32).reshape(1, HID),
        item_table,
        tower_in,
        tower_out,
        cross_weights,
        mlp_in,
        mlp_mid,
    )


def solution(mesh):
    in_specs = (
        P("req", "score", None, None, None),
        P(None, "req", "score"),
        P(("req", "score"), None),
        P(None, "req", None),
        P(None, "score"),
        P("score", None),
        P(),
        P(),
        P(),
        P(),
    )
    return jax.shard_map(
        on_device,
        mesh=mesh,
        in_specs=in_specs,
        out_specs=P(None, "req", "score"),
        check_vma=False,
    )
```

time: 160 us -> 68 us (0.42)
  blocking collectives: 74.8 us -> 0 us
  Pallas kernels: 0 us -> 61.7 us
  matrix products: 25.8 us -> 0 us
  local copies, waits for them, and re-layouts: 26.5 us -> 3.93 us
  starting transfers between devices: 15.8 us -> 0 us
  waiting for transfers between devices: 10.9 us -> 0 us
  other arithmetic: 5.15 us -> 1.29 us
    psum x1 -> x0, blocking collectives: 74.8 us -> none  [on_device(): user = lax.psum(partial_user, 'score').astype(jnp.bfloat16)]
    pallas_call x0 -> x1, Pallas kernels: none -> 61.7 us  [on_device(): pl.pallas_call(kernel, out_shape=jax.ShapeDtypeStruct((WINDOWS, REQ_ROWS,...]
    dot_general x5 -> x0, matrix products: 25.8 us -> none  [the longest x1 13.4 us: on_device(): logits = jnp.dot(second, mlp_out, preferred_element_type=jnp.float32)]
    all_to_all x2 -> x0, starting transfers between devices: 15.8 us -> none  [the longest x1 11.1 us: on_device(): lax.all_to_all(send_rows, ('req', 'score'), split_axis=0, concat_axis=0,...]
    gather x3 -> x0, local copies, waits for them, and re-layouts: 13.2 us -> none  [the longest x2 9.31 us: on_device(): jnp.take(item_table, jnp.maximum(lax.all_to_all(send_rows, ('req', 'score...]
    all_to_all x2 -> x0, waiting for transfers between devices: 10.9 us -> none  [the longest x1 10.9 us: on_device(): lax.all_to_all(send_rows, ('req', 'score'), split_axis=0, concat_axis=0,...]
    scatter x1 -> x0, local copies, waits for them, and re-layouts: 4.32 us -> none  [on_device(): send_rows.at[flat_index].set(local_rows.reshape(-1))]
    reshape x5 -> x1, local copies, waits for them, and re-layouts: 4.21 us -> 1.36 us  [on_device(): local_rows.reshape(WINDOWS, BLOCK)]
  transfers between devices with their start and end apart: 2 -> 0, of which waited for: 1 -> 0; matrix products, arithmetic and copies ran while one was open for 0% -> 0% of each run, Pallas kernels for 0% -> 0%
where the time goes in v1:
time: 68 us; the launch traced here: 66.9 us
  Pallas kernels  61.7 us (91%)
  local copies, waits for them, and re-layouts  3.93 us (6%)
  other arithmetic  1.29 us (2%)
    pallas_call x1, Pallas kernels, on_device(): pl.pallas_call(kernel, out_shape=jax.ShapeDtypeStruct((WINDOWS, REQ_ROWS,...  61.7 us
    unnamed x2, local copies, waits for them, and re-layouts  2.57 us
    reshape x1, local copies, waits for them, and re-layouts, on_device(): local_rows.reshape(WINDOWS, BLOCK)  1.36 us

profile of v1, /device:TPU:0, one launch (start us, length us, event | category | flops | bytes accessed | tf_op | source)
XLA Modules:
  0.0 66.9 jit_solution(16949332144866160024)
XLA Ops:
  0.0 1.3 %copy.13 = s32[1,1,4,256,1]{3,2,4,1,0:T(4,128)} copy(s32[1,1,4,256,1]{3,4,2,1,0:T(1,128)} %param.10) | data formatting | bytes 8192
  1.3 1.4 %reshape.12.rows_ref = s32[4,256]{1,0:T(4,128)} reshape(s32[4,4,64]{2,1,0:T(4,128)} %param.11) | data formatting | bytes 8192 | tf_op jit(solution)/shard_map/reshape | solution.py:308
  2.6 1.3 %reshape.15 = f32[2048]{0:T(1024)} convert(bf16[2048]{0:T(1024)(128)(2,1)} %param.19) | non-fusion elementwise | flops 2048 | bytes 12288 | tf_op jit(solution)/shard_map/reshape | solution.py:310
  3.9 61.7 %shard_map.100 = f32[4,4,64]{2,1,0:T(4,128)} custom-call(s32[4,256]{1,0:T(4,128)} %bitcast.5, s32[4,256]{1,0:T(4,128)} %reshape.12.rows_ref, bf16[4,4,1024]{2,1,0:T(4,128)(2,1)} %feats_ref.1, f32[1,2048]{1,0:T(1,128)} %bitcast.4, bf16[16384,256]{1,0:T(8,128)(2,1)} %table_hbm.1, bf16[1024,128]{1,0:T(8,128)(2,1)} %tin_hbm.1, bf16[128,256]{1,0:T(8,128)(2,1)} %tout_hbm.1, ...), custom_call_target="tpu_custom_call" | custom-call | flops 13500000256 | bytes 21000000 | tf_op jit(solution)/shard_map/pallas_call | solution.py:267
  65.6 1.3 %copy.15 = f32[4,4,64]{2,1,0:T(4,128)} copy(f32[4,4,64]{2,1,0:T(4,128)} %shard_map.100) | data formatting | bytes 8192

commit v2 on v1

--- a/solution.py
+++ b/solution.py
@@ -27,14 +27,27 @@
 BF16 = jnp.bfloat16
 
 
-def peer(step):
+def for_peers(visit, first=1):
     req, score = lax.axis_index("req"), lax.axis_index("score")
-    turn = (step * 37) % 128
-    z = (score % 4 + turn % 4) % 4
-    y = (score // 4 + (turn // 4) % 4) % 4
-    core = (req % 2 + (turn // 16) % 2) % 2
-    x = (req // 2 + turn // 32) % 4
-    return x * 2 + core, y * 4 + z
+    core = req % 2
+    x, y, z = req // 2, score // 4, score % 4
+    xs = [((x + d) % 4) * 2 for d in range(4)]
+    ys = [((y + d) % 4) * 4 for d in range(4)]
+    zs = tuple((z + d) % 4 for d in range(4))
+
+    def step(o, zs, start):
+        here = jnp.where(o < 4, core, 1 - core)
+        cores = (here, 1 - here)
+        group = []
+        for k in range(start, 16):
+            dx, turn = k % 4, k // 4
+            dy = (turn + dx) % 4
+            group.append((k, xs[dx] + cores[(dx + turn) % 2], ys[dy] + zs[(turn + 2 * dx) % 4]))
+        visit(o, group)
+        return zs[1:] + zs[:1]
+
+    zs = step(0, zs, first)
+    lax.fori_loop(1, 8, lambda o, zs: step(o, zs, 0), zs)
 
 
 def kernel(
@@ -42,7 +55,7 @@
     table_hbm, tin_hbm, tout_hbm, cross_hbm, win_hbm, wmid_hbm,
     logits_ref,
     table, table32, tin, tout, cross, win, wmid,
-    ask, asked, asked_s, stage, give, got, part, parts, pick, first,
+    out_w, ask, asked, asked_s, stage, give, got, part, parts, pick, first,
     load_sem, weight_sem, own_sem, ask_send, ask_recv, user_send, user_recv, row_send, row_recv,
 ):
     req, score = lax.axis_index("req"), lax.axis_index("score")
@@ -69,12 +82,11 @@
 
     barrier = pltpu.get_barrier_semaphore()
 
-    def greet(step, carry):
-        to_req, to_score = peer(step)
-        pl.semaphore_signal(barrier, inc=1, device_id=(to_req, to_score), device_id_type=MESH)
-        return carry
-
-    lax.fori_loop(1, OWNERS, greet, 0)
+    def greet(o, group):
+        for _, to_req, to_score in group:
+            pl.semaphore_signal(barrier, inc=1, device_id=(to_req, to_score), device_id_type=MESH)
+
+    for_peers(greet)
 
     tri_row = lax.broadcasted_iota(jnp.int32, (BLOCK, BLOCK), 0)
     tri_col = lax.broadcasted_iota(jnp.int32, (BLOCK, BLOCK), 1)
@@ -84,8 +96,8 @@
     low_sum = jnp.zeros((OWNERS, 128), F32)
     places = []
     for w in range(WINDOWS):
-        owner = owner_ref[pl.ds(w, 1), :]
-        rows = rows_ref[pl.ds(w, 1), :]
+        owner = owner_ref[w]
+        rows = jnp.concatenate([rows_ref[w, r:r + 1, :] for r in range(REQ_ROWS)], axis=1)
         hot = jnp.where(owner_iota == owner, 1.0, 0.0)
         hot16 = hot.astype(BF16)
         before = jnp.dot(hot16, earlier, preferred_element_type=F32)
@@ -102,19 +114,18 @@
 
     pl.semaphore_wait(barrier, OWNERS - 1)
 
-    def send_ask(step, carry):
-        to_req, to_score = peer(step)
-        pltpu.make_async_remote_copy(
-            src_ref=ask.at[to_req * 16 + to_score],
-            dst_ref=asked.at[me],
-            send_sem=ask_send,
-            recv_sem=ask_recv,
-            device_id=(to_req, to_score),
-            device_id_type=MESH,
-        ).start()
-        return carry
-
-    lax.fori_loop(1, OWNERS, send_ask, 0)
+    def send_ask(o, group):
+        for _, to_req, to_score in group:
+            pltpu.make_async_remote_copy(
+                src_ref=ask.at[to_req * 16 + to_score],
+                dst_ref=asked.at[me],
+                send_sem=ask_send,
+                recv_sem=ask_recv,
+                device_id=(to_req, to_score),
+                device_id_type=MESH,
+            ).start()
+
+    for_peers(send_ask)
     asked[pl.ds(me, 1)] = ask[pl.ds(me, 1)]
 
     for copy in small:
@@ -162,40 +173,35 @@
     to_smem = pltpu.make_async_copy(asked, asked_s, own_sem.at[0])
     to_smem.start()
 
-    def clear(step, carry):
-        stage[pl.ds(pl.multiple_of(step * 64, 64), 64), :] = jnp.zeros((64, 128), F32)
-        return carry
-
-    lax.fori_loop(0, 2 * OWNERS * 2 * SLOTS // 64, clear, 0)
+    stage[...] = jnp.zeros_like(stage)
     to_smem.wait()
 
-    def look_up(half, to):
-        base = pl.multiple_of((half * OWNERS + to) * 2 * SLOTS, 2 * SLOTS)
+    def look_up(half, to, slot, k):
+        base = k * 2 * SLOTS
         for s in range(USED):
             at = jnp.clip(asked_s[to, 0, half * USED + s], 0, 2 * ROWS - 2)
-            stage[pl.ds(base + 2 * s, 2), :] = table32[pl.ds(at, 2), :]
-        give[half, to, 0:SLOTS, :] = stage[pl.ds(base, SLOTS, stride=2), :].astype(BF16)
-        give[half, to, SLOTS:2 * SLOTS, :] = stage[pl.ds(base + 1, SLOTS, stride=2), :].astype(BF16)
+            stage[base + 2 * s:base + 2 * s + 2, :] = table32[pl.ds(at, 2), :]
+        give[half, slot, 0:SLOTS, :] = stage[pl.ds(base, SLOTS, stride=2), :].astype(BF16)
+        give[half, slot, SLOTS:2 * SLOTS, :] = stage[pl.ds(base + 1, SLOTS, stride=2), :].astype(BF16)
 
     for half in range(2):
 
-        def send_rows(step, carry):
-            to_req, to_score = peer(step)
-            to = to_req * 16 + to_score
-            look_up(half, to)
-            pltpu.make_async_remote_copy(
-                src_ref=give.at[half, to],
-                dst_ref=got.at[half, me],
-                send_sem=row_send.at[half],
-                recv_sem=row_recv.at[half],
-                device_id=(to_req, to_score),
-                device_id_type=MESH,
-            ).start()
-            return carry
-
-        lax.fori_loop(1, OWNERS, send_rows, 0)
-        look_up(half, me)
-        got[half, pl.ds(me, 1)] = give[half, pl.ds(me, 1)]
+        def send_rows(o, group):
+            for k, to_req, to_score in group:
+                look_up(half, to_req * 16 + to_score, o * 16 + k, k)
+            for k, to_req, to_score in group:
+                pltpu.make_async_remote_copy(
+                    src_ref=give.at[half, o * 16 + k],
+                    dst_ref=got.at[half, me],
+                    send_sem=row_send.at[half],
+                    recv_sem=row_recv.at[half],
+                    device_id=(to_req, to_score),
+                    device_id_type=MESH,
+                ).start()
+
+        for_peers(send_rows)
+        look_up(half, me, 0, 0)
+        got[half, pl.ds(me, 1)] = give[half, 0:1]
 
     fifteen = parts.at[pl.ds(0, 15)]
     pltpu.make_async_copy(fifteen, fifteen, user_recv).wait()
@@ -204,6 +210,7 @@
         copy.wait()
     user_mixed = jnp.dot(user, cross[0, ITEM:, :], preferred_element_type=F32)
     user32 = user.astype(F32)
+    out_w[...] = out_w_ref[...].astype(F32)
 
     def spread(rows, half):
         width = rows.shape[1]
@@ -242,8 +249,9 @@
         def deep_mid(n, total):
             columns = pl.ds(pl.multiple_of(n * 256, 256), 256)
             value = jnp.dot(first[...], wmid[:, columns], preferred_element_type=F32)
-            second = jnp.maximum(value, 0.0).astype(BF16).astype(F32) * out_w_ref[:, columns]
-            return total + second[:, :128] + second[:, 128:]
+            second = jnp.maximum(value, 0.0).astype(BF16).astype(F32)
+            total += second[:, :128] * out_w[pl.ds(2 * n, 1), :]
+            return total + second[:, 128:] * out_w[pl.ds(2 * n + 1, 1), :]
 
         total = lax.fori_loop(0, HID // 256, deep_mid, jnp.zeros((HALF, 128), F32))
         scores = jnp.sum(total.T, axis=0, keepdims=True)
@@ -277,10 +285,11 @@
             pltpu.VMEM((CROSS, 512, 512), BF16),
             pltpu.VMEM((512, HID), BF16),
             pltpu.VMEM((HID, HID), BF16),
+            pltpu.VMEM((HID // 128, 128), F32),
             pltpu.VMEM((OWNERS, 1, 128), jnp.int32),
             pltpu.VMEM((OWNERS, 1, 128), jnp.int32),
             pltpu.SMEM((OWNERS, 1, 128), jnp.int32),
-            pltpu.VMEM((2 * OWNERS * 2 * SLOTS + 8, 128), F32),
+            pltpu.VMEM((16 * 2 * SLOTS + 8, 128), F32),
             pltpu.VMEM((2, OWNERS, 2 * SLOTS, 128), BF16),
             pltpu.VMEM((2, OWNERS, 2 * SLOTS, 128), BF16),
             pltpu.VMEM((16, USER), F32),
@@ -304,10 +313,10 @@
             flops=13_500_000_000, bytes_accessed=21_000_000, transcendentals=0
         ),
     )(
-        owner_ids.reshape(WINDOWS, BLOCK),
-        local_rows.reshape(WINDOWS, BLOCK),
+        owner_ids.reshape(WINDOWS, 1, BLOCK),
+        local_rows,
         user_feats,
-        mlp_out.astype(F32).reshape(1, HID),
+        mlp_out.reshape(HID // 128, 128),
         item_table,
         tower_in,
         tower_out,

time: 68 us -> 52.8 us (0.78); the launches traced: 66.9 us -> 52.6 us
  Pallas kernels: 61.7 us -> 51.3 us
  local copies, waits for them, and re-layouts: 3.93 us -> 1.3 us
  other arithmetic: 1.29 us -> 0 us
    pallas_call x1, Pallas kernels: 61.7 us -> 51.3 us  [on_device(): pl.pallas_call(kernel, out_shape=jax.ShapeDtypeStruct((WINDOWS, REQ_ROWS,...]
    reshape x1 -> x0, local copies, waits for them, and re-layouts: 1.36 us -> none  [on_device(): local_rows.reshape(WINDOWS, BLOCK)]
    reshape x1 -> x0, other arithmetic: 1.29 us -> none  [on_device(): mlp_out.astype(F32).reshape(1, HID)]
    unnamed x2 -> x1, local copies, waits for them, and re-layouts: 2.57 us -> 1.3 us
where the time goes in v2:
time: 52.8 us; the launch traced here: 52.6 us
  Pallas kernels  51.3 us (97%)
  local copies, waits for them, and re-layouts  1.3 us (2%)
    pallas_call x1, Pallas kernels, on_device(): pl.pallas_call(kernel, out_shape=jax.ShapeDtypeStruct((WINDOWS, REQ_ROWS,...  51.3 us
    unnamed x1, local copies, waits for them, and re-layouts  1.3 us

profile of v2, /device:TPU:0, one launch (start us, length us, event | category | flops | bytes accessed | tf_op | source)
XLA Modules:
  0.0 52.6 jit_solution(14263196369904375310)
XLA Ops:
  0.0 51.3 %shard_map.100 = f32[4,4,64]{2,1,0:T(4,128)} custom-call(s32[4,1,256]{2,1,0:T(1,128)} %bitcast.2, s32[4,4,64]{2,1,0:T(4,128)} %rows_ref.1, bf16[4,4,1024]{2,1,0:T(4,128)(2,1)} %feats_ref.1, bf16[16,128]{1,0:T(8,128)(2,1)} %bitcast.3, bf16[16384,256]{1,0:T(8,128)(2,1)} %table_hbm.1, bf16[1024,128]{1,0:T(8,128)(2,1)} %tin_hbm.1, bf16[128,256]{1,0:T(8,128)(2,1)} %tout_hbm.1, ...), custom_call_target="tpu_custom_call" | custom-call | flops 13500000256 | bytes 21000000 | tf_op jit(solution)/shard_map/pallas_call | solution.py:275
  51.3 1.3 %copy.12 = f32[4,4,64]{2,1,0:T(4,128)} copy(f32[4,4,64]{2,1,0:T(4,128)} %shard_map.100) | data formatting | bytes 8192

commit v3 on v2

--- a/solution.py
+++ b/solution.py
@@ -184,9 +184,35 @@
         give[half, slot, 0:SLOTS, :] = stage[pl.ds(base, SLOTS, stride=2), :].astype(BF16)
         give[half, slot, SLOTS:2 * SLOTS, :] = stage[pl.ds(base + 1, SLOTS, stride=2), :].astype(BF16)
 
-    for half in range(2):
-
-        def send_rows(o, group):
+    def find_rows(half):
+        def visit(o, group):
+            for k, to_req, to_score in group:
+                look_up(half, to_req * 16 + to_score, o * 16 + k, k)
+
+        for_peers(visit)
+        look_up(half, me, 0, 0)
+        got[half, pl.ds(me, 1)] = give[half, 0:1]
+
+    def send_rows(half):
+        def visit(o, group):
+            for k, to_req, to_score in group:
+                pltpu.make_async_remote_copy(
+                    src_ref=give.at[half, o * 16 + k],
+                    dst_ref=got.at[half, me],
+                    send_sem=row_send.at[half],
+                    recv_sem=row_recv.at[half],
+                    device_id=(to_req, to_score),
+                    device_id_type=MESH,
+                ).start()
+
+        for_peers(visit)
+
+    def wait_rows(half, sem):
+        arrived = got.at[half, pl.ds(0, OWNERS - 1)]
+        pltpu.make_async_copy(arrived, arrived, sem.at[half]).wait()
+
+    def find_and_send(half):
+        def visit(o, group):
             for k, to_req, to_score in group:
                 look_up(half, to_req * 16 + to_score, o * 16 + k, k)
             for k, to_req, to_score in group:
@@ -199,9 +225,12 @@
                     device_id_type=MESH,
                 ).start()
 
-        for_peers(send_rows)
+        for_peers(visit)
         look_up(half, me, 0, 0)
         got[half, pl.ds(me, 1)] = give[half, 0:1]
+
+    find_and_send(0)
+    find_rows(1)
 
     fifteen = parts.at[pl.ds(0, 15)]
     pltpu.make_async_copy(fifteen, fifteen, user_recv).wait()
@@ -212,6 +241,9 @@
     user32 = user.astype(F32)
     out_w[...] = out_w_ref[...].astype(F32)
 
+    wait_rows(0, row_send)
+    send_rows(1)
+
     def spread(rows, half):
         width = rows.shape[1]
         return jnp.concatenate(
@@ -220,8 +252,7 @@
         )
 
     for half in range(2):
-        arrived = got.at[half, pl.ds(0, OWNERS - 1)]
-        pltpu.make_async_copy(arrived, arrived, row_recv.at[half]).wait()
+        wait_rows(half, row_recv)
         left = got[half, :, 0:SLOTS, :].reshape(OWNERS * SLOTS, 128)
         right = got[half, :, SLOTS:2 * SLOTS, :].reshape(OWNERS * SLOTS, 128)
         found = jnp.concatenate([left, right], axis=1)
@@ -244,7 +275,7 @@
             first[:, columns] = jnp.maximum(value, 0.0).astype(BF16)
             return carry
 
-        lax.fori_loop(0, HID // 256, deep_in, 0)
+        lax.fori_loop(0, HID // 256, deep_in, 0, unroll=True)
 
         def deep_mid(n, total):
             columns = pl.ds(pl.multiple_of(n * 256, 256), 256)
@@ -253,16 +284,16 @@
             total += second[:, :128] * out_w[pl.ds(2 * n, 1), :]
             return total + second[:, 128:] * out_w[pl.ds(2 * n + 1, 1), :]
 
-        total = lax.fori_loop(0, HID // 256, deep_mid, jnp.zeros((HALF, 128), F32))
+        total = lax.fori_loop(
+            0, HID // 256, deep_mid, jnp.zeros((HALF, 128), F32), unroll=True
+        )
         scores = jnp.sum(total.T, axis=0, keepdims=True)
         for q in range(8):
             logits_ref[half * 2 + q // 4, pl.ds(q % 4, 1), :] = scores[:, q * CAND:(q + 1) * CAND]
 
     pltpu.make_async_copy(everything, everything, ask_send).wait()
     pltpu.make_async_copy(fifteen, fifteen, user_send).wait()
-    for half in range(2):
-        arrived = got.at[half, pl.ds(0, OWNERS - 1)]
-        pltpu.make_async_copy(arrived, arrived, row_send.at[half]).wait()
+    wait_rows(1, row_send)
 
 
 def on_device(

time: 52.8 us -> 46.3 us (0.88)
  Pallas kernels: 51.3 us -> 44.6 us
    pallas_call x1, Pallas kernels: 51.3 us -> 44.6 us  [on_device(): pl.pallas_call(kernel, out_shape=jax.ShapeDtypeStruct((WINDOWS, REQ_ROWS,...]
where the time goes in v3:
time: 46.3 us; the launch traced here: 45.9 us
  Pallas kernels  44.6 us (96%)
  local copies, waits for them, and re-layouts  1.3 us (3%)
    pallas_call x1, Pallas kernels, on_device(): pl.pallas_call(kernel, out_shape=jax.ShapeDtypeStruct((WINDOWS, REQ_ROWS,...  44.6 us
    unnamed x1, local copies, waits for them, and re-layouts  1.3 us

profile of v3, /device:TPU:0, one launch (start us, length us, event | category | flops | bytes accessed | tf_op | source)
XLA Modules:
  0.0 45.9 jit_solution(9424192495656448727)
XLA Ops:
  0.0 44.6 %shard_map.100 = f32[4,4,64]{2,1,0:T(4,128)} custom-call(s32[4,1,256]{2,1,0:T(1,128)} %bitcast.2, s32[4,4,64]{2,1,0:T(4,128)} %rows_ref.1, bf16[4,4,1024]{2,1,0:T(4,128)(2,1)} %feats_ref.1, bf16[16,128]{1,0:T(8,128)(2,1)} %bitcast.3, bf16[16384,256]{1,0:T(8,128)(2,1)} %table_hbm.1, bf16[1024,128]{1,0:T(8,128)(2,1)} %tin_hbm.1, bf16[128,256]{1,0:T(8,128)(2,1)} %tout_hbm.1, ...), custom_call_target="tpu_custom_call" | custom-call | flops 13500000256 | bytes 21000000 | tf_op jit(solution)/shard_map/pallas_call | solution.py:306
  44.6 1.3 %copy.12 = f32[4,4,64]{2,1,0:T(4,128)} copy(f32[4,4,64]{2,1,0:T(4,128)} %shard_map.100) | data formatting | bytes 8192

commit v4 on v2

v4 whole, which is shorter than its diff:
```python
import functools

import jax
import jax.numpy as jnp
from jax import lax
from jax.experimental import pallas as pl
from jax.experimental.pallas import tpu as pltpu
from jax.sharding import PartitionSpec as P

CROSS = 3
WINDOWS = 4
BLOCK = 256
REQ_ROWS = 4
CAND = 64
MOST = 3
OWNERS = 128
ROWS = 16384
ITEM = 256
USER = 256
HID = 2048
HALF = 2 * BLOCK
SLOTS = 8
PARTS = ((0, MOST), (MOST, MOST), (2 * MOST, 2 * MOST))
CHUNKS = 8
MESH = pl.DeviceIdType.MESH
F32 = jnp.float32
BF16 = jnp.bfloat16


TURNS = (
    (2, 2), (2, 1), (2, 3), (1, 2), (3, 2), (1, 1), (1, 3), (3, 1),
    (3, 3), (2, 0), (0, 2), (1, 0), (3, 0), (0, 1), (0, 3), (0, 0),
)


def for_peers(visit):
    req, score = lax.axis_index("req"), lax.axis_index("score")
    core = req % 2
    x, y, z = req // 2, score // 4, score % 4
    xs = [((x + d) % 4) * 2 for d in range(4)]
    ys = [((y + d) % 4) * 4 for d in range(4)]
    zs = tuple((z + d) % 4 for d in (2, 2, 1, 1, 3, 3, 0, 0))

    def step(o, carry, last):
        zs, cores = carry
        visit(o, [
            (k, xs[dx] + cores[0], ys[dy] + zs[0]) for k, (dx, dy) in enumerate(TURNS[:last])
        ])
        return zs[1:] + zs[:1], cores[::-1]

    step(7, lax.fori_loop(0, 7, lambda o, carry: step(o, carry, 16), (zs, (1 - core, core))), 15)


def kernel(
    owner_hbm, rows_hbm, feats_hbm, out_w_hbm,
    table_hbm, tin_hbm, tout_hbm, cross_hbm, win_hbm, wmid_hbm,
    logits_ref,
    table, table32, tin, tout, cross, win, wmid,
    owner_ref, rows_ref, feats_ref, out_w_ref,
    out_w, ask, asked, asked_s, stage, give1, got1, give2, got2, part, parts, pick, first,
    load_sem, weight_sem, own_sem, ask_send, ask_recv, user_send, user_recv, row_send, row_recv,
):
    req, score = lax.axis_index("req"), lax.axis_index("score")
    me = req * 16 + score
    chunk = ROWS // CHUNKS

    ids = [
        pltpu.make_async_copy(owner_hbm, owner_ref, own_sem.at[1]),
        pltpu.make_async_copy(rows_hbm, rows_ref, own_sem.at[2]),
    ]
    small = [
        pltpu.make_async_copy(feats_hbm, feats_ref, own_sem.at[3]),
        pltpu.make_async_copy(out_w_hbm, out_w_ref, own_sem.at[4]),
        pltpu.make_async_copy(tin_hbm, tin, weight_sem.at[0]),
        pltpu.make_async_copy(tout_hbm, tout, weight_sem.at[1]),
    ]
    large = [
        pltpu.make_async_copy(cross_hbm, cross, weight_sem.at[2]),
        pltpu.make_async_copy(win_hbm, win, weight_sem.at[3]),
        pltpu.make_async_copy(wmid_hbm, wmid, weight_sem.at[4]),
    ]
    loads = [
        pltpu.make_async_copy(
            table_hbm.at[pl.ds(k * chunk, chunk)], table.at[pl.ds(k * chunk, chunk)], load_sem.at[k]
        )
        for k in range(CHUNKS)
    ]
    for copy in ids + small + loads + large:
        copy.start()

    barrier = pltpu.get_barrier_semaphore()

    def greet(o, group):
        for _, to_req, to_score in group:
            pl.semaphore_signal(barrier, inc=1, device_id=(to_req, to_score), device_id_type=MESH)

    for_peers(greet)

    tri_row = lax.broadcasted_iota(jnp.int32, (BLOCK, BLOCK), 0)
    tri_col = lax.broadcasted_iota(jnp.int32, (BLOCK, BLOCK), 1)
    earlier = jnp.where(tri_row < tri_col, 1.0, 0.0).astype(BF16)
    owner_iota = lax.broadcasted_iota(jnp.int32, (OWNERS, BLOCK), 0)
    high_sum = jnp.zeros((OWNERS, 128), F32)
    low_sum = jnp.zeros((OWNERS, 128), F32)
    places = []
    for copy in ids:
        copy.wait()
    for w in range(WINDOWS):
        owner = owner_ref[w]
        rows = jnp.concatenate([rows_ref[w, r:r + 1, :] for r in range(REQ_ROWS)], axis=1)
        hot = jnp.where(owner_iota == owner, 1.0, 0.0)
        hot16 = hot.astype(BF16)
        before = jnp.dot(hot16, earlier, preferred_element_type=F32)
        slot = jnp.sum(before * hot, axis=0, keepdims=True).astype(jnp.int32)
        at_slot = owner_iota == slot + w * MOST
        high = jnp.where(at_slot, (rows // 128).astype(F32), 0.0).astype(BF16)
        low = jnp.where(at_slot, (rows % 128).astype(F32), 0.0).astype(BF16)
        contract = (((1,), (1,)), ((), ()))
        high_sum += lax.dot_general(hot16, high, contract, preferred_element_type=F32)
        low_sum += lax.dot_general(hot16, low, contract, preferred_element_type=F32)
        if w < 2:
            places += [owner * SLOTS + 2 * slot, owner * SLOTS + 2 * slot + 1]
        else:
            places.append(owner * SLOTS + slot + (w % 2) * MOST)
    asks = (high_sum * 128.0 + low_sum).astype(jnp.int32) * 2
    ask[...] = asks.reshape(OWNERS, 1, 128)

    for copy in small:
        copy.wait()
    feats = jnp.concatenate([feats_ref[w].astype(F32) for w in range(WINDOWS)], axis=0).astype(BF16)
    hidden = jnp.maximum(jnp.dot(feats, tin[...], preferred_element_type=F32), 0.0).astype(BF16)
    part[...] = jnp.dot(hidden, tout[...], preferred_element_type=F32)

    pl.semaphore_wait(barrier, OWNERS - 1)

    def send_ask(o, group):
        for _, to_req, to_score in group:
            pltpu.make_async_remote_copy(
                src_ref=ask.at[to_req * 16 + to_score],
                dst_ref=asked.at[me],
                send_sem=ask_send,
                recv_sem=ask_recv,
                device_id=(to_req, to_score),
                device_id_type=MESH,
            ).start()

    for_peers(send_ask)
    asked[pl.ds(me, 1)] = ask[pl.ds(me, 1)]

    def send_part(step, carry):
        pltpu.make_async_remote_copy(
            src_ref=part,
            dst_ref=parts.at[score],
            send_sem=user_send,
            recv_sem=user_recv,
            device_id=(req, (score + step) % 16),
            device_id_type=MESH,
        ).start()
        return carry

    lax.fori_loop(1, 16, send_part, 0)
    parts[pl.ds(score, 1)] = part[...][None]

    for k in range(CHUNKS):
        loads[k].wait()

        def widen(step, carry):
            base = pl.multiple_of(k * chunk + step * 64, 64)
            block = table[pl.ds(base, 64), :].astype(F32)
            table32[pl.ds(2 * base, 64, stride=2), :] = block[:, :128]
            table32[pl.ds(2 * base + 1, 64, stride=2), :] = block[:, 128:]
            return carry

        lax.fori_loop(0, chunk // 64, widen, 0, unroll=4)

    everything = asked.at[pl.ds(0, OWNERS - 1)]
    pltpu.make_async_copy(everything, everything, ask_recv).wait()
    to_smem = pltpu.make_async_copy(asked, asked_s, own_sem.at[0])
    to_smem.start()

    stage[...] = jnp.zeros_like(stage)
    to_smem.wait()

    def look_up(part_of, to, slot, k):
        base = k * 2 * SLOTS
        first_slot, count = PARTS[part_of]
        for n in range(count):
            at = jnp.clip(asked_s[to, 0, first_slot + n], 0, 2 * ROWS - 2)
            stage[base + 2 * n:base + 2 * n + 2, :] = table32[pl.ds(at, 2), :]
        if part_of < 2:
            give1[part_of, slot] = stage[base:base + SLOTS, :].astype(BF16)
        else:
            give2[slot, 0:SLOTS, :] = stage[pl.ds(base, SLOTS, stride=2), :].astype(BF16)
            give2[slot, SLOTS:2 * SLOTS, :] = stage[pl.ds(base + 1, SLOTS, stride=2), :].astype(BF16)

    gives = [give1.at[0], give1.at[1], give2]
    gots = [got1.at[0], got1.at[1], got2]

    def send_row(part_of, slot, to_req, to_score):
        pltpu.make_async_remote_copy(
            src_ref=gives[part_of].at[slot],
            dst_ref=gots[part_of].at[me],
            send_sem=row_send.at[part_of],
            recv_sem=row_recv.at[part_of],
            device_id=(to_req, to_score),
            device_id_type=MESH,
        ).start()

    def wait_rows(part_of, sem):
        arrived = gots[part_of].at[pl.ds(0, OWNERS - 1)]
        pltpu.make_async_copy(arrived, arrived, sem.at[part_of]).wait()

    def find_and_send(o, group):
        for k, to_req, to_score in group:
            look_up(0, to_req * 16 + to_score, o * 16 + k, k)
        for k, to_req, to_score in group:
            send_row(0, o * 16 + k, to_req, to_score)

    for_peers(find_and_send)

    for part_of in (1, 2):

        def find(o, group):
            for k, to_req, to_score in group:
                look_up(part_of, to_req * 16 + to_score, o * 16 + k, k)

        def send(o, group):
            for k, to_req, to_score in group:
                send_row(part_of, o * 16 + k, to_req, to_score)

        for_peers(find)
        wait_rows(part_of - 1, row_send)
        for_peers(send)

    for part_of in range(3):
        look_up(part_of, me, OWNERS - 1, 15)
    got1[:, pl.ds(me, 1)] = give1[:, OWNERS - 1:OWNERS]
    got2[pl.ds(me, 1)] = give2[OWNERS - 1:OWNERS]

    place = jnp.concatenate(places + [jnp.zeros((2, BLOCK), jnp.int32)], axis=0)
    place_t = place.T
    lane = lax.broadcasted_iota(jnp.int32, (BLOCK, OWNERS * SLOTS), 1)
    for w in range(6):
        pick[w * BLOCK:(w + 1) * BLOCK, :] = jnp.where(
            lane == place_t[:, w:w + 1], 1.0, 0.0
        ).astype(BF16)

    fifteen = parts.at[pl.ds(0, 15)]
    pltpu.make_async_copy(fifteen, fifteen, user_recv).wait()
    user = jnp.sum(parts[...], axis=0).astype(BF16)
    for copy in large:
        copy.wait()
    user_mixed = jnp.dot(user, cross[0, ITEM:, :], preferred_element_type=F32)
    user32 = user.astype(F32)
    out_w[...] = out_w_ref[...].astype(F32)

    def spread(rows, requests):
        width = rows.shape[1]
        return jnp.concatenate(
            [jnp.broadcast_to(rows[q:q + 1], (CAND, width)) for q in requests], axis=0
        )

    def dense(embedded, requests, deep):
        base = jnp.concatenate([embedded, spread(user32, requests)], axis=1)
        mixed = jnp.dot(
            embedded.astype(BF16), cross[0, :ITEM, :], preferred_element_type=F32
        ) + spread(user_mixed, requests)
        state = base * mixed + base
        for layer in range(1, CROSS):
            mixed = jnp.dot(state.astype(BF16), cross[layer], preferred_element_type=F32)
            state = base * mixed + state
        state16 = state.astype(BF16)

        def deep_in(n, carry):
            columns = pl.ds(pl.multiple_of(n * 256, 256), 256)
            value = jnp.dot(state16, win[:, columns], preferred_element_type=F32)
            deep[:, columns] = jnp.maximum(value, 0.0).astype(BF16)
            return carry

        lax.fori_loop(0, HID // 256, deep_in, 0, unroll=True)

        def deep_mid(n, total):
            columns = pl.ds(pl.multiple_of(n * 256, 256), 256)
            value = jnp.dot(deep[...], wmid[:, columns], preferred_element_type=F32)
            second = jnp.maximum(value, 0.0).astype(BF16).astype(F32)
            total += second[:, :128] * out_w[pl.ds(2 * n, 1), :]
            return total + second[:, 128:] * out_w[pl.ds(2 * n + 1, 1), :]

        total = jnp.zeros((len(requests) * CAND, 128), F32)
        total = lax.fori_loop(0, HID // 256, deep_mid, total, unroll=True)
        scores = jnp.sum(total.T, axis=0, keepdims=True)
        for n, q in enumerate(requests):
            logits_ref[q // 4, q % 4:q % 4 + 1, :] = scores[:, n * CAND:(n + 1) * CAND]

    for w in range(2):
        wait_rows(w, row_recv)
        found = got1[w].reshape(OWNERS * SLOTS, 128)
        sides = jnp.dot(
            pick[2 * w * BLOCK:2 * (w + 1) * BLOCK, :], found, preferred_element_type=F32
        )
        embedded = jnp.concatenate([sides[:BLOCK], sides[BLOCK:]], axis=1)
        dense(embedded, range(4 * w, 4 * w + 4), first.at[pl.ds(w * BLOCK, BLOCK)])
    wait_rows(2, row_recv)
    left = got2[:, 0:SLOTS, :].reshape(OWNERS * SLOTS, 128)
    right = got2[:, SLOTS:2 * SLOTS, :].reshape(OWNERS * SLOTS, 128)
    found = jnp.concatenate([left, right], axis=1)
    embedded = jnp.dot(pick[4 * BLOCK:, :], found, preferred_element_type=F32)
    dense(embedded, range(8, 16), first)

    pltpu.make_async_copy(everything, everything, ask_send).wait()
    pltpu.make_async_copy(fifteen, fifteen, user_send).wait()
    wait_rows(2, row_send)


def on_device(
    owner_ids, local_rows, item_table, user_feats, tower_in, tower_out,
    cross_weights, mlp_in, mlp_mid, mlp_out,
):
    vmem = pl.BlockSpec(memory_space=pltpu.VMEM)
    hbm = pl.BlockSpec(memory_space=pl.ANY)
    dma = pltpu.SemaphoreType.DMA
    return pl.pallas_call(
        kernel,
        out_shape=jax.ShapeDtypeStruct((WINDOWS, REQ_ROWS, CAND), F32),
        in_specs=[hbm] * 10,
        out_specs=vmem,
        scratch_shapes=[
            pltpu.VMEM((ROWS, ITEM), BF16),
            pltpu.VMEM((2 * ROWS + 8, 128), F32),
            pltpu.VMEM((1024, 128), BF16),
            pltpu.VMEM((128, USER), BF16),
            pltpu.VMEM((CROSS, 512, 512), BF16),
            pltpu.VMEM((512, HID), BF16),
            pltpu.VMEM((HID, HID), BF16),
            pltpu.VMEM((WINDOWS, 1, BLOCK), jnp.int32),
            pltpu.VMEM((WINDOWS, REQ_ROWS, CAND), jnp.int32),
            pltpu.VMEM((WINDOWS, REQ_ROWS, 1024), BF16),
            pltpu.VMEM((HID // 128, 128), BF16),
            pltpu.VMEM((HID // 128, 128), F32),
            pltpu.VMEM((OWNERS, 1, 128), jnp.int32),
            pltpu.VMEM((OWNERS, 1, 128), jnp.int32),
            pltpu.SMEM((OWNERS, 1, 128), jnp.int32),
            pltpu.VMEM((16 * 2 * SLOTS + 8, 128), F32),
            pltpu.VMEM((2, OWNERS, SLOTS, 128), BF16),
            pltpu.VMEM((2, OWNERS, SLOTS, 128), BF16),
            pltpu.VMEM((OWNERS, 2 * SLOTS, 128), BF16),
            pltpu.VMEM((OWNERS, 2 * SLOTS, 128), BF16),
            pltpu.VMEM((16, USER), F32),
            pltpu.VMEM((16, 16, USER), F32),
            pltpu.VMEM((6 * BLOCK, OWNERS * SLOTS), BF16),
            pltpu.VMEM((HALF, HID), BF16),
            dma((CHUNKS,)),
            dma((5,)),
            dma((5,)),
            dma,
            dma,
            dma,
            dma,
            dma((3,)),
            dma((3,)),
        ],
        compiler_params=pltpu.CompilerParams(
            collective_id=0, has_side_effects=True, vmem_limit_bytes=60 * 1024 * 1024
        ),
        cost_estimate=pl.CostEstimate(
            flops=13_500_000_000, bytes_accessed=21_000_000, transcendentals=0
        ),
    )(
        owner_ids.reshape(WINDOWS, 1, BLOCK),
        local_rows,
        user_feats,
        mlp_out.reshape(HID // 128, 128),
        item_table,
        tower_in,
        tower_out,
        cross_weights,
        mlp_in,
        mlp_mid,
    )


def solution(mesh):
    in_specs = (
        P("req", "score", None, None, None),
        P(None, "req", "score"),
        P(("req", "score"), None),
        P(None, "req", None),
        P(None, "score"),
        P("score", None),
        P(),
        P(),
        P(),
        P(),
    )
    return jax.shard_map(
        on_device,
        mesh=mesh,
        in_specs=in_specs,
        out_specs=P(None, "req", "score"),
        check_vma=False,
    )
```

time: 52.8 us -> 43.6 us (0.83)
  Pallas kernels: 51.3 us -> 42.2 us
    pallas_call x1, Pallas kernels: 51.3 us -> 42.2 us  [on_device(): pl.pallas_call(kernel, out_shape=jax.ShapeDtypeStruct((WINDOWS, REQ_ROWS,...]
where the time goes in v4:
time: 43.6 us; the launch traced here: 43.5 us
  Pallas kernels  42.2 us (97%)
  local copies, waits for them, and re-layouts  1.3 us (3%)
    pallas_call x1, Pallas kernels, on_device(): pl.pallas_call(kernel, out_shape=jax.ShapeDtypeStruct((WINDOWS, REQ_ROWS,...  42.2 us
    unnamed x1, local copies, waits for them, and re-layouts  1.3 us

profile of v4, /device:TPU:0, one launch (start us, length us, event | category | flops | bytes accessed | tf_op | source)
XLA Modules:
  0.0 43.5 jit_solution(10357496389327258177)
XLA Ops:
  0.0 42.2 %shard_map.100 = f32[4,4,64]{2,1,0:T(4,128)} custom-call(s32[4,1,256]{2,1,0:T(1,128)} %bitcast.2, s32[4,4,64]{2,1,0:T(4,128)} %rows_hbm.1, bf16[4,4,1024]{2,1,0:T(4,128)(2,1)} %feats_hbm.1, bf16[16,128]{1,0:T(8,128)(2,1)} %bitcast.3, bf16[16384,256]{1,0:T(8,128)(2,1)} %table_hbm.1, bf16[1024,128]{1,0:T(8,128)(2,1)} %tin_hbm.1, bf16[128,256]{1,0:T(8,128)(2,1)} %tout_hbm.1, ...), custom_call_target="tpu_custom_call" | custom-call | flops 13500000256 | bytes 21000000 | tf_op jit(solution)/shard_map/pallas_call | solution.py:322
  42.2 1.3 %copy.12 = f32[4,4,64]{2,1,0:T(4,128)} copy(f32[4,4,64]{2,1,0:T(4,128)} %shard_map.100) | data formatting | bytes 8192

commit v5 on v4

--- a/solution.py
+++ b/solution.py
@@ -218,25 +218,21 @@
 
     for_peers(find_and_send)
 
-    for part_of in (1, 2):
-
-        def find(o, group):
+    def find_rows(part_of):
+        def visit(o, group):
             for k, to_req, to_score in group:
                 look_up(part_of, to_req * 16 + to_score, o * 16 + k, k)
 
-        def send(o, group):
+        for_peers(visit)
+
+    def send_rows(part_of):
+        def visit(o, group):
             for k, to_req, to_score in group:
                 send_row(part_of, o * 16 + k, to_req, to_score)
 
-        for_peers(find)
-        wait_rows(part_of - 1, row_send)
-        for_peers(send)
-
-    for part_of in range(3):
-        look_up(part_of, me, OWNERS - 1, 15)
-    got1[:, pl.ds(me, 1)] = give1[:, OWNERS - 1:OWNERS]
-    got2[pl.ds(me, 1)] = give2[OWNERS - 1:OWNERS]
-
+        for_peers(visit)
+
+    find_rows(1)
     place = jnp.concatenate(places + [jnp.zeros((2, BLOCK), jnp.int32)], axis=0)
     place_t = place.T
     lane = lax.broadcasted_iota(jnp.int32, (BLOCK, OWNERS * SLOTS), 1)
@@ -245,6 +241,13 @@
             lane == place_t[:, w:w + 1], 1.0, 0.0
         ).astype(BF16)
 
+    wait_rows(0, row_send)
+    send_rows(1)
+    find_rows(2)
+    for part_of in range(3):
+        look_up(part_of, me, OWNERS - 1, 15)
+    got1[:, pl.ds(me, 1)] = give1[:, OWNERS - 1:OWNERS]
+    got2[pl.ds(me, 1)] = give2[OWNERS - 1:OWNERS]
     fifteen = parts.at[pl.ds(0, 15)]
     pltpu.make_async_copy(fifteen, fifteen, user_recv).wait()
     user = jnp.sum(parts[...], axis=0).astype(BF16)
@@ -253,6 +256,9 @@
     user_mixed = jnp.dot(user, cross[0, ITEM:, :], preferred_element_type=F32)
     user32 = user.astype(F32)
     out_w[...] = out_w_ref[...].astype(F32)
+
+    wait_rows(1, row_send)
+    send_rows(2)
 
     def spread(rows, requests):
         width = rows.shape[1]

time: 43.6 us -> 43.1 us (0.989); the launches traced: 43.5 us -> 42.4 us
  Pallas kernels: 42.2 us -> 41.1 us
    pallas_call x1, Pallas kernels: 42.2 us -> 41.1 us  [on_device(): pl.pallas_call(kernel, out_shape=jax.ShapeDtypeStruct((WINDOWS, REQ_ROWS,...]
where the time goes in v5:
time: 43.1 us; the launch traced here: 42.4 us
  Pallas kernels  41.1 us (95%)
  local copies, waits for them, and re-layouts  1.3 us (3%)
    pallas_call x1, Pallas kernels, on_device(): pl.pallas_call(kernel, out_shape=jax.ShapeDtypeStruct((WINDOWS, REQ_ROWS,...  41.1 us
    unnamed x1, local copies, waits for them, and re-layouts  1.3 us

profile of v5, /device:TPU:0, one launch (start us, length us, event | category | flops | bytes accessed | tf_op | source)
XLA Modules:
  0.0 42.4 jit_solution(15296324219907056233)
XLA Ops:
  0.0 41.1 %shard_map.100 = f32[4,4,64]{2,1,0:T(4,128)} custom-call(s32[4,1,256]{2,1,0:T(1,128)} %bitcast.2, s32[4,4,64]{2,1,0:T(4,128)} %rows_hbm.1, bf16[4,4,1024]{2,1,0:T(4,128)(2,1)} %feats_hbm.1, bf16[16,128]{1,0:T(8,128)(2,1)} %bitcast.3, bf16[16384,256]{1,0:T(8,128)(2,1)} %table_hbm.1, bf16[1024,128]{1,0:T(8,128)(2,1)} %tin_hbm.1, bf16[128,256]{1,0:T(8,128)(2,1)} %tout_hbm.1, ...), custom_call_target="tpu_custom_call" | custom-call | flops 13500000256 | bytes 21000000 | tf_op jit(solution)/shard_map/pallas_call | solution.py:328
  41.1 1.3 %copy.12 = f32[4,4,64]{2,1,0:T(4,128)} copy(f32[4,4,64]{2,1,0:T(4,128)} %shard_map.100) | data formatting | bytes 8192

commit v6 on v5

--- a/solution.py
+++ b/solution.py
@@ -85,7 +85,7 @@
         )
         for k in range(CHUNKS)
     ]
-    for copy in ids + small + loads + large:
+    for copy in ids:
         copy.start()
 
     barrier = pltpu.get_barrier_semaphore()
@@ -95,6 +95,8 @@
             pl.semaphore_signal(barrier, inc=1, device_id=(to_req, to_score), device_id_type=MESH)
 
     for_peers(greet)
+    for copy in small + loads + large:
+        copy.start()
 
     tri_row = lax.broadcasted_iota(jnp.int32, (BLOCK, BLOCK), 0)
     tri_col = lax.broadcasted_iota(jnp.int32, (BLOCK, BLOCK), 1)
@@ -125,12 +127,6 @@
     asks = (high_sum * 128.0 + low_sum).astype(jnp.int32) * 2
     ask[...] = asks.reshape(OWNERS, 1, 128)
 
-    for copy in small:
-        copy.wait()
-    feats = jnp.concatenate([feats_ref[w].astype(F32) for w in range(WINDOWS)], axis=0).astype(BF16)
-    hidden = jnp.maximum(jnp.dot(feats, tin[...], preferred_element_type=F32), 0.0).astype(BF16)
-    part[...] = jnp.dot(hidden, tout[...], preferred_element_type=F32)
-
     pl.semaphore_wait(barrier, OWNERS - 1)
 
     def send_ask(o, group):
@@ -146,6 +142,12 @@
 
     for_peers(send_ask)
     asked[pl.ds(me, 1)] = ask[pl.ds(me, 1)]
+
+    for copy in small:
+        copy.wait()
+    feats = jnp.concatenate([feats_ref[w].astype(F32) for w in range(WINDOWS)], axis=0).astype(BF16)
+    hidden = jnp.maximum(jnp.dot(feats, tin[...], preferred_element_type=F32), 0.0).astype(BF16)
+    part[...] = jnp.dot(hidden, tout[...], preferred_element_type=F32)
 
     def send_part(step, carry):
         pltpu.make_async_remote_copy(

time: 43.1 us -> 42.7 us (level)
  no operation moved by 1% of the time
where the time goes in v6:
time: 42.7 us; the launch traced here: 42.1 us
  Pallas kernels  40.8 us (96%)
  local copies, waits for them, and re-layouts  1.3 us (3%)
    pallas_call x1, Pallas kernels, on_device(): pl.pallas_call(kernel, out_shape=jax.ShapeDtypeStruct((WINDOWS, REQ_ROWS,...  40.8 us
    unnamed x1, local copies, waits for them, and re-layouts  1.3 us

profile of v6, /device:TPU:0, one launch (start us, length us, event | category | flops | bytes accessed | tf_op | source)
XLA Modules:
  0.0 42.1 jit_solution(10965379754269814308)
XLA Ops:
  0.0 40.8 %shard_map.100 = f32[4,4,64]{2,1,0:T(4,128)} custom-call(s32[4,1,256]{2,1,0:T(1,128)} %bitcast.2, s32[4,4,64]{2,1,0:T(4,128)} %rows_hbm.1, bf16[4,4,1024]{2,1,0:T(4,128)(2,1)} %feats_hbm.1, bf16[16,128]{1,0:T(8,128)(2,1)} %bitcast.3, bf16[16384,256]{1,0:T(8,128)(2,1)} %table_hbm.1, bf16[1024,128]{1,0:T(8,128)(2,1)} %tin_hbm.1, bf16[128,256]{1,0:T(8,128)(2,1)} %tout_hbm.1, ...), custom_call_target="tpu_custom_call" | custom-call | flops 13500000256 | bytes 21000000 | tf_op jit(solution)/shard_map/pallas_call | solution.py:330
  40.8 1.3 %copy.12 = f32[4,4,64]{2,1,0:T(4,128)} copy(f32[4,4,64]{2,1,0:T(4,128)} %shard_map.100) | data formatting | bytes 8192
